TPU v7x, 128 devices: a whole 4x4x4 slice. The times are simulated.
128 devices in a mesh: dp: 8 (over z, core), ctx: 16 (over y, x).
Axes of the slice: x: 4, y: 4, z: 4, core: 2. Of those that a mesh axis runs over, the one named last changes fastest.
Arguments:
- attn_in: bfloat16 [8, 2048, 4096], P('dp', 'ctx'), may hold values from -6 to 6
- attn_mix: bfloat16 [8, 2048, 4096], P('dp', 'ctx'), may hold values from -6 to 6
- mlp_in: bfloat16 [8, 2048, 4096], P('dp', 'ctx'), may hold values from -6 to 6
- mlp_act: bfloat16 [8, 2048, 14336], P('dp', 'ctx'), may hold values from -6 to 6
- grad_query: bfloat16 [8, 2048, 4096], P('dp', 'ctx'), may hold values from -0.19921875 to 0.19921875
- grad_key: bfloat16 [8, 2048, 1024], P('dp', 'ctx'), may hold values from -0.19921875 to 0.19921875
- grad_value: bfloat16 [8, 2048, 1024], P('dp', 'ctx'), may hold values from -0.19921875 to 0.19921875
- grad_output: bfloat16 [8, 2048, 4096], P('dp', 'ctx'), may hold values from -0.19921875 to 0.19921875
- grad_gate: bfloat16 [8, 2048, 14336], P('dp', 'ctx'), may hold values from -0.19921875 to 0.19921875
- grad_up: bfloat16 [8, 2048, 14336], P('dp', 'ctx'), may hold values from -0.19921875 to 0.19921875
- grad_down: bfloat16 [8, 2048, 4096], P('dp', 'ctx'), may hold values from -0.19921875 to 0.19921875
- proj_attn: bfloat16 [4096, 64], replicated, may hold values from -0.09375 to 0.09375
- proj_mix: bfloat16 [4096, 64], replicated, may hold values from -0.09375 to 0.09375
- proj_mlp: bfloat16 [4096, 64], replicated, may hold values from -0.09375 to 0.09375
- proj_act: bfloat16 [14336, 64], replicated, may hold values from -0.046875 to 0.046875
- proj_query: bfloat16 [4096, 64], replicated, may hold values from -0.09375 to 0.09375
- proj_key: bfloat16 [1024, 64], replicated, may hold values from -0.1875 to 0.1875
- proj_value: bfloat16 [1024, 64], replicated, may hold values from -0.1875 to 0.1875
- proj_output: bfloat16 [4096, 64], replicated, may hold values from -0.09375 to 0.09375
- proj_gate: bfloat16 [14336, 64], replicated, may hold values from -0.046875 to 0.046875
- proj_upward: bfloat16 [14336, 64], replicated, may hold values from -0.046875 to 0.046875
- proj_down: bfloat16 [4096, 64], replicated, may hold values from -0.09375 to 0.09375
- seq_counts: int32 [8], P('dp'), may hold values from 128 to 2048, as said below
- example_ids: int32 [8], replicated, may hold values from 0 to 7, each once
Outputs:
- store: float32 [8, 7, 4096], P('dp', None, 'ctx')
Inputs may be any that keep to these rules, and one draw needn't show every extreme that they name: `seq_counts`: every count is a multiple of 128; some sequence has all 2048 tokens. `example_ids`: a permutation: every store row receives exactly one sequence.
All inputs are finite; a program needn't handle non-finite values.
Results may differ from a plain program's by a relative error of at most 0.004.
Values sent between devices are 32-bit elements; how exact they have to be, the bound alone decides.
No kernel may reach another device: no remote copies, remote signals or barrier semaphores. Data moves between devices by JAX's collectives and lax.ppermute only.
A program may use at most 128 MiB of HBM per device.

v0:
```python
import jax
import jax.numpy as jnp
from jax import lax
from jax.sharding import PartitionSpec as P


def project_rows(acts, projection):
    return jnp.dot(acts[0], projection, preferred_element_type=jnp.float32).astype(jnp.bfloat16)


def outer_sum(grads_proj, inputs_proj):
    product = lax.dot_general(
        grads_proj, inputs_proj, (((0,), (0,)), ((), ())), preferred_element_type=jnp.float32
    )
    return product.reshape(-1)


def reduce_positions(values):
    summed = lax.psum(values, "ctx")
    width = values.shape[2] // lax.axis_size("ctx")
    return lax.dynamic_slice_in_dim(summed, lax.axis_index("ctx") * width, width, 2)


def pick_owned(gathered, example_ids):
    owner = lax.axis_index("dp")
    weights = (example_ids == owner).astype(jnp.float32)
    return jnp.sum(weights[:, None, None] * gathered, axis=0, keepdims=True)


def shards(
    attn_in,
    attn_mix,
    mlp_in,
    mlp_act,
    grad_query,
    grad_key,
    grad_value,
    grad_output,
    grad_gate,
    grad_up,
    grad_down,
    proj_attn,
    proj_mix,
    proj_mlp,
    proj_act,
    proj_query,
    proj_key,
    proj_value,
    proj_output,
    proj_gate,
    proj_upward,
    proj_down,
    seq_counts,
    example_ids,
):
    length_dev = attn_in.shape[1]
    first_pos = lax.axis_index("ctx") * length_dev
    limit_pos = seq_counts[0]
    live_rows = (first_pos + jnp.arange(length_dev, dtype=jnp.int32) < limit_pos).astype(
        jnp.bfloat16
    )[:, None]
    attn_p = project_rows(attn_in, proj_attn)
    mix_p = project_rows(attn_mix, proj_mix)
    mlp_p = project_rows(mlp_in, proj_mlp)
    act_p = project_rows(mlp_act, proj_act)
    pairs = [
        (grad_query, proj_query, attn_p),
        (grad_key, proj_key, attn_p),
        (grad_value, proj_value, attn_p),
        (grad_output, proj_output, mix_p),
        (grad_gate, proj_gate, mlp_p),
        (grad_up, proj_upward, mlp_p),
        (grad_down, proj_down, act_p),
    ]
    sketches = [
        outer_sum(project_rows(grads, projection) * live_rows, inputs_proj)
        for grads, projection, inputs_proj in pairs
    ]
    partial_sum = jnp.stack(sketches, axis=0)[None]
    shared = reduce_positions(partial_sum)
    gathered = lax.all_gather(shared, "dp", axis=0, tiled=True)
    return pick_owned(gathered, example_ids)


def solution(mesh):
    return jax.shard_map(
        shards,
        mesh=mesh,
        in_specs=(
            P("dp", "ctx", None),
            P("dp", "ctx", None),
            P("dp", "ctx", None),
            P("dp", "ctx", None),
            P("dp", "ctx", None),
            P("dp", "ctx", None),
            P("dp", "ctx", None),
            P("dp", "ctx", None),
            P("dp", "ctx", None),
            P("dp", "ctx", None),
            P("dp", "ctx", None),
            P(),
            P(),
            P(),
            P(),
            P(),
            P(),
            P(),
            P(),
            P(),
            P(),
            P(),
            P("dp"),
            P(),
        ),
        out_specs=P("dp", None, "ctx"),
        check_vma=False,
    )
```

profile of v0, /device:TPU:1, one launch (start us, length us, event | category | flops | bytes accessed | tf_op | source)
XLA Modules:
  0.0 140.8 jit_solution(12949452242620769150)
XLA Ops:
  6.5 0.0 copy-start
  6.5 0.0 all-reduce.2.cloned.1.call-start
  7.3 1.8 %convolution_convert_fusion.6 = bf16[128,64]{0,1:T(8,128)(2,1)S(1)} fusion(bf16[4096,64]{0,1:T(8,128)(2,1)} %param.37, bf16[1,128,4096]{2,1,0:T(8,128)(2,1)} %param.26), kind=kOutput, calls=%fused_computation.29 | convolution fusion | flops 67117056 | bytes 1589248 | tf_op jit(solution)/shard_map/dot_general | solution.py:8
  9.2 0.0 copy-done
  9.2 3.3 %fusion.22 = f32[64,64]{1,0:T(8,128)S(1)} fusion(bf16[128,64]{0,1:T(8,128)(2,1)S(1)} %convolution_convert_fusion.6, bf16[14336,64]{0,1:T(8,128)(2,1)S(1)} %copy-done, bf16[1,128,14336]{2,1,0:T(8,128)(2,1)} %param.33, bf16[128]{0:T(256)(128)(2,1)S(1)} %compare_convert_fusion), kind=kOutput, calls=%fused_computation.17 | convolution fusion | flops 235945984 | bytes 5538048 | tf_op jit(solution)/shard_map/dot_general | solution.py:12
  12.5 0.0 copy-start.2
  12.5 0.1 stack_reshape.26
  12.6 0.0 copy-start.1
  12.6 4.0 %fusion.28 = f32[64,64]{1,0:T(8,128)S(1)} fusion(bf16[128,64]{0,1:T(8,128)(2,1)S(1)} %convolution_convert_fusion.6, bf16[14336,64]{0,1:T(8,128)(2,1)} %param.43, bf16[1,128,14336]{2,1,0:T(8,128)(2,1)} %param.32, bf16[128]{0:T(256)(128)(2,1)S(1)} %compare_convert_fusion), kind=kOutput, calls=%fused_computation.19 | convolution fusion | flops 235945984 | bytes 5538048 | tf_op jit(solution)/shard_map/dot_general | solution.py:12
  16.6 0.1 stack_reshape.25
  16.7 0.0 copy-done.2
  16.7 1.7 %convolution_convert_fusion.7 = bf16[128,64]{0,1:T(8,128)(2,1)S(1)} fusion(bf16[4096,64]{0,1:T(8,128)(2,1)S(1)} %copy-done.2, bf16[1,128,4096]{2,1,0:T(8,128)(2,1)} %param.24), kind=kOutput, calls=%fused_computation.30 | convolution fusion | flops 67117056 | bytes 1589248 | tf_op jit(solution)/shard_map/dot_general | solution.py:8
  18.4 0.0 copy-start.3
  18.4 1.4 %fusion.38 = f32[64,64]{1,0:T(8,128)S(1)} fusion(bf16[128,64]{0,1:T(8,128)(2,1)S(1)} %convolution_convert_fusion.7, bf16[1024,64]{0,1:T(8,128)(2,1)} %param.41, bf16[1,128,1024]{2,1,0:T(8,128)(2,1)} %param.30, bf16[128]{0:T(256)(128)(2,1)S(1)} %compare_convert_fusion), kind=kOutput, calls=%fused_computation.28 | convolution fusion | flops 17842176 | bytes 426240 | tf_op jit(solution)/shard_map/dot_general | solution.py:12
  19.8 0.1 stack_reshape.23
  20.0 1.4 fusion.36
  21.3 0.1 stack_reshape.22
  21.4 0.0 copy-done.1
  21.4 1.6 %fusion.31 = f32[64,64]{1,0:T(8,128)S(1)} fusion(bf16[128,64]{0,1:T(8,128)(2,1)S(1)} %convolution_convert_fusion.7, bf16[4096,64]{0,1:T(8,128)(2,1)} %param.39, bf16[1,128,4096]{2,1,0:T(8,128)(2,1)S(1)} %copy-done.1, bf16[128]{0:T(256)(128)(2,1)S(1)} %compare_convert_fusion), kind=kOutput, calls=%fused_computation.21 | convolution fusion | flops 68173824 | bytes 1605888 | tf_op jit(solution)/shard_map/dot_general | solution.py:12
  23.1 0.1 stack_reshape.21
  23.2 1.8 %convolution_convert_fusion.1 = bf16[128,64]{1,0:T(8,128)(2,1)S(1)} fusion(bf16[4096,64]{0,1:T(8,128)(2,1)} %param.36, bf16[1,128,4096]{2,1,0:T(8,128)(2,1)} %param.25), kind=kOutput, calls=%fused_computation.10 | convolution fusion | flops 67117056 | bytes 1589248 | tf_op jit(solution)/shard_map/dot_general | solution.py:8
  25.0 0.0 copy-done.3
  25.0 1.8 %fusion.33 = f32[64,64]{1,0:T(8,128)S(1)} fusion(bf16[128,64]{1,0:T(8,128)(2,1)S(1)} %convolution_convert_fusion.1, bf16[4096,64]{0,1:T(8,128)(2,1)S(1)} %copy-done.3, bf16[1,128,4096]{2,1,0:T(8,128)(2,1)} %param.31, bf16[128]{0:T(256)(128)(2,1)S(1)} %compare_convert_fusion), kind=kOutput, calls=%fused_computation.23 | convolution fusion | flops 68173824 | bytes 1605888 | tf_op jit(solution)/shard_map/dot_general | solution.py:12
  26.8 0.1 stack_reshape.24
  26.9 0.0 copy-start.4
  26.9 1.8 %fusion.34 = bf16[128,64]{1,0:T(8,128)(2,1)S(1)} fusion(bf16[4096,64]{0,1:T(8,128)(2,1)} %param.45, bf16[1,128,4096]{2,1,0:T(8,128)(2,1)} %param.34, bf16[128]{0:T(256)(128)(2,1)S(1)} %compare_convert_fusion), kind=kOutput, calls=%fused_computation.24 | convolution fusion | flops 67125248 | bytes 1589504 | tf_op jit(solution)/shard_map/dot_general | solution.py:8
  28.7 3.8 %fusion.16 = f32[64,64]{1,0:T(8,128)S(1)} fusion(bf16[128,64]{1,0:T(8,128)(2,1)S(1)} %fusion.34, bf16[14336,64]{0,1:T(8,128)(2,1)} %param.38, bf16[1,128,14336]{2,1,0:T(8,128)(2,1)} %param.27), kind=kOutput, calls=%fused_computation.15 | convolution fusion | flops 235937792 | bytes 5537792 | tf_op jit(solution)/shard_map/dot_general | solution.py:12
  32.5 0.1 stack_reshape.27
  32.6 0.8 stack.3
  33.4 0.0 all-reduce.2.cloned.1.call-update
  33.5 0.0 copy-done.4
  33.5 83.8 %all-reduce.2.cloned.1.call-done = f32[1,7,4096]{2,1,0:T(8,128)} async-done(((f32[1,7,4096]{2,1,0:T(8,128)}), f32[1,7,4096]{2,1,0:T(8,128)}) %all-reduce.2.cloned.1.call-update) | async-done | bytes 114704 | tf_op jit(solution)/shard_map/psum | solution.py:19
  117.3 0.7 constant_dynamic-slice_fusion
  118.0 15.2 %all_gather.3 = f32[8,7,256]{2,1,0:T(8,128)S(1)} all-gather(f32[1,7,256]{2,1,0:T(8,128)S(1)} %constant_dynamic-slice_fusion), channel_id=1, replica_groups=mesh['dp'=8,'ctx'=16] {'dp'}, dimensions={0}, use_global_device_ids=true | all-gather | bytes 64512 | tf_op jit(solution)/shard_map/all_gather | solution.py:81
  133.3 0.1 multiply_reduce_fusion
  133.3 0.6 broadcast_in_dim.9
  (2 shorter events, 0.0 us)
Async XLA Ops:
  6.5 2.7 %copy-start = (bf16[14336,64]{0,1:T(8,128)(2,1)S(1)}, bf16[14336,64]{0,1:T(8,128)(2,1)}, u32[]{:S(2)}) copy-start(bf16[14336,64]{0,1:T(8,128)(2,1)} %param.44) | copy-start | bytes 5505028
  6.5 110.8 %all-reduce.2.cloned.1.call-start = ((), (), s32[]{:S(2)}) async-start(), calls=%async_computation | async-start | bytes 262144 | tf_op jit(solution)/shard_map/psum | solution.py:19
  12.5 4.2 %copy-start.2 = (bf16[4096,64]{0,1:T(8,128)(2,1)S(1)}, bf16[4096,64]{0,1:T(8,128)(2,1)}, u32[]{:S(2)}) copy-start(bf16[4096,64]{0,1:T(8,128)(2,1)} %param.35) | copy-start | bytes 1572868
  12.6 8.8 %copy-start.1 = (bf16[1,128,4096]{2,1,0:T(8,128)(2,1)S(1)}, bf16[1,128,4096]{2,1,0:T(8,128)(2,1)}, u32[]{:S(2)}) copy-start(bf16[1,128,4096]{2,1,0:T(8,128)(2,1)} %param.28) | copy-start | bytes 3145732
  18.4 6.6 %copy-start.3 = (bf16[4096,64]{0,1:T(8,128)(2,1)S(1)}, bf16[4096,64]{0,1:T(8,128)(2,1)}, u32[]{:S(2)}) copy-start(bf16[4096,64]{0,1:T(8,128)(2,1)} %param.42) | copy-start | bytes 1572868
  26.9 6.6 %copy-start.4 = (s32[8]{0:T(128)S(1)}, s32[8]{0:T(128)}, u32[]{:S(2)}) copy-start(s32[8]{0:T(128)} %param.47) | copy-start | bytes 100
Sparse Core Ops, SparseCore 0:
  33.6 83.6 all-reduce.1
where the time goes:
time: 141 us
  waiting for transfers between devices  83.8 us (59%)
  matrix products  24.4 us (17%)
  blocking collectives  15.2 us (11%)
  between operations  14.3 us (10%)
  local copies, waits for them, and re-layouts  2.84 us (2%)
    psum x1, waiting for transfers between devices, reduce_positions(): summed = lax.psum(values, 'ctx')  83.8 us
    dot_general x7, matrix products, outer_sum(): lax.dot_general(grads_proj, inputs_proj, (((0,), (0,)), ((), ())), prefer...  17.3 us
    all_gather x1, blocking collectives, shards(): gathered = lax.all_gather(shared, 'dp', axis=0, tiled=True)  15.2 us
    dot_general x4, matrix products, project_rows(): jnp.dot(acts[0], projection, preferred_element_type=jnp.float32)  7.1 us
  transfers between devices with their start and end apart: 1, of which 1 were waited for; matrix products, arithmetic and copies ran while one was open for 0% of the time, Pallas kernels for 0%

commit v1 on v0

--- a/solution.py
+++ b/solution.py
@@ -16,7 +16,7 @@
 
 
 def reduce_positions(values):
-    summed = lax.psum(values, "ctx")
+    summed = jnp.sum(lax.all_gather(values, "ctx"), axis=0)
     width = values.shape[2] // lax.axis_size("ctx")
     return lax.dynamic_slice_in_dim(summed, lax.axis_index("ctx") * width, width, 2)
 

time: 141 us -> 105 us (0.74)
  waiting for transfers between devices: 83.8 us -> 47.3 us
  other arithmetic: 0.09 us -> 1.83 us
    psum x1 -> x0, waiting for transfers between devices: 83.8 us -> none  [reduce_positions(): summed = lax.psum(values, 'ctx')]
    all_gather x0 -> x1, waiting for transfers between devices: none -> 47.3 us  [reduce_positions(): summed = jnp.sum(lax.all_gather(values, 'ctx'), axis=0)]
    reduce_sum x0 -> x1, other arithmetic: none -> 1.74 us  [reduce_positions(): summed = jnp.sum(lax.all_gather(values, 'ctx'), axis=0)]
where the time goes in v1:
time: 105 us; the launch traced here: 104 us
  waiting for transfers between devices  47.3 us (45%)
  matrix products  24.2 us (23%)
  blocking collectives  14.5 us (14%)
  between operations  14.4 us (14%)
  local copies, waits for them, and re-layouts  2.16 us (2%)
  other arithmetic  1.83 us (2%)
    all_gather x1, waiting for transfers between devices, reduce_positions(): summed = jnp.sum(lax.all_gather(values, 'ctx'), axis=0)  47.3 us
    dot_general x7, matrix products, outer_sum(): lax.dot_general(grads_proj, inputs_proj, (((0,), (0,)), ((), ())), prefer...  17.4 us
    all_gather x1, blocking collectives, shards(): gathered = lax.all_gather(shared, 'dp', axis=0, tiled=True)  14.5 us
    dot_general x4, matrix products, project_rows(): jnp.dot(acts[0], projection, preferred_element_type=jnp.float32)  6.79 us
  transfers between devices with their start and end apart: 1, of which 1 were waited for; matrix products, arithmetic and copies ran while one was open for 0% of the time, Pallas kernels for 0%

profile of v1, /device:TPU:1, one launch (start us, length us, event | category | flops | bytes accessed | tf_op | source)
XLA Modules:
  0.0 104.4 jit_solution(16195129717624067858)
XLA Ops:
  6.5 0.0 copy-start
  6.5 0.0 all-gather.6.cloned.1.call-start
  7.3 1.8 %convolution_convert_fusion.6 = bf16[128,64]{0,1:T(8,128)(2,1)S(1)} fusion(bf16[4096,64]{0,1:T(8,128)(2,1)} %param.37, bf16[1,128,4096]{2,1,0:T(8,128)(2,1)} %param.26), kind=kOutput, calls=%fused_computation.29 | convolution fusion | flops 67117056 | bytes 1589248 | tf_op jit(solution)/shard_map/dot_general | solution.py:8
  9.2 0.0 copy-done
  9.2 3.3 %fusion.22 = f32[64,64]{1,0:T(8,128)S(1)} fusion(bf16[128,64]{0,1:T(8,128)(2,1)S(1)} %convolution_convert_fusion.6, bf16[14336,64]{0,1:T(8,128)(2,1)S(1)} %copy-done, bf16[1,128,14336]{2,1,0:T(8,128)(2,1)} %param.33, bf16[128]{0:T(256)(128)(2,1)S(1)} %compare_convert_fusion), kind=kOutput, calls=%fused_computation.17 | convolution fusion | flops 235945984 | bytes 5538048 | tf_op jit(solution)/shard_map/dot_general | solution.py:12
  12.5 0.1 stack_reshape.26
  12.6 0.0 copy-start.3
  12.6 3.9 %fusion.28 = f32[64,64]{1,0:T(8,128)S(1)} fusion(bf16[128,64]{0,1:T(8,128)(2,1)S(1)} %convolution_convert_fusion.6, bf16[14336,64]{0,1:T(8,128)(2,1)} %param.43, bf16[1,128,14336]{2,1,0:T(8,128)(2,1)} %param.32, bf16[128]{0:T(256)(128)(2,1)S(1)} %compare_convert_fusion), kind=kOutput, calls=%fused_computation.19 | convolution fusion | flops 235945984 | bytes 5538048 | tf_op jit(solution)/shard_map/dot_general | solution.py:12
  16.5 0.0 copy-start.1
  16.5 0.1 stack_reshape.25
  16.6 0.0 copy-done.3
  16.7 1.8 %convolution_convert_fusion.7 = bf16[128,64]{0,1:T(8,128)(2,1)S(1)} fusion(bf16[4096,64]{0,1:T(8,128)(2,1)S(1)} %copy-done.3, bf16[1,128,4096]{2,1,0:T(8,128)(2,1)} %param.24), kind=kOutput, calls=%fused_computation.30 | convolution fusion | flops 67117056 | bytes 1589248 | tf_op jit(solution)/shard_map/dot_general | solution.py:8
  18.4 0.0 copy-start.4
  18.4 1.4 %fusion.38 = f32[64,64]{1,0:T(8,128)S(1)} fusion(bf16[128,64]{0,1:T(8,128)(2,1)S(1)} %convolution_convert_fusion.7, bf16[1024,64]{0,1:T(8,128)(2,1)} %param.41, bf16[1,128,1024]{2,1,0:T(8,128)(2,1)} %param.30, bf16[128]{0:T(256)(128)(2,1)S(1)} %compare_convert_fusion), kind=kOutput, calls=%fused_computation.28 | convolution fusion | flops 17842176 | bytes 426240 | tf_op jit(solution)/shard_map/dot_general | solution.py:12
  19.9 0.1 stack_reshape.23
  20.0 1.4 %fusion.36 = f32[64,64]{1,0:T(8,128)S(1)} fusion(bf16[128,64]{0,1:T(8,128)(2,1)S(1)} %convolution_convert_fusion.7, bf16[1024,64]{0,1:T(8,128)(2,1)} %param.40, bf16[1,128,1024]{2,1,0:T(8,128)(2,1)} %param.29, bf16[128]{0:T(256)(128)(2,1)S(1)} %compare_convert_fusion), kind=kOutput, calls=%fused_computation.26 | convolution fusion | flops 17842176 | bytes 426240 | tf_op jit(solution)/shard_map/dot_general | solution.py:12
  21.3 0.1 stack_reshape.22
  21.5 0.0 copy-done.1
  21.5 1.6 %fusion.31 = f32[64,64]{1,0:T(8,128)S(1)} fusion(bf16[128,64]{0,1:T(8,128)(2,1)S(1)} %convolution_convert_fusion.7, bf16[4096,64]{0,1:T(8,128)(2,1)} %param.39, bf16[1,128,4096]{2,1,0:T(8,128)(2,1)S(1)} %copy-done.1, bf16[128]{0:T(256)(128)(2,1)S(1)} %compare_convert_fusion), kind=kOutput, calls=%fused_computation.21 | convolution fusion | flops 68173824 | bytes 1605888 | tf_op jit(solution)/shard_map/dot_general | solution.py:12
  23.1 0.0 copy-start.2
  23.1 0.1 stack_reshape.21
  23.2 0.0 copy-done.4
  23.2 1.7 %convolution_convert_fusion.1 = bf16[128,64]{1,0:T(8,128)(2,1)S(1)} fusion(bf16[4096,64]{0,1:T(8,128)(2,1)S(1)} %copy-done.4, bf16[1,128,4096]{2,1,0:T(8,128)(2,1)} %param.25), kind=kOutput, calls=%fused_computation.10 | convolution fusion | flops 67117056 | bytes 1589248 | tf_op jit(solution)/shard_map/dot_general | solution.py:8
  24.9 1.9 %fusion.33 = f32[64,64]{1,0:T(8,128)S(1)} fusion(bf16[128,64]{1,0:T(8,128)(2,1)S(1)} %convolution_convert_fusion.1, bf16[4096,64]{0,1:T(8,128)(2,1)} %param.42, bf16[1,128,4096]{2,1,0:T(8,128)(2,1)} %param.31, bf16[128]{0:T(256)(128)(2,1)S(1)} %compare_convert_fusion), kind=kOutput, calls=%fused_computation.23 | convolution fusion | flops 68173824 | bytes 1605888 | tf_op jit(solution)/shard_map/dot_general | solution.py:12
  26.9 0.1 stack_reshape.24
  27.0 0.0 copy-done.2
  27.0 1.5 %fusion.34 = bf16[128,64]{1,0:T(8,128)(2,1)S(1)} fusion(bf16[4096,64]{0,1:T(8,128)(2,1)} %param.45, bf16[1,128,4096]{2,1,0:T(8,128)(2,1)S(1)} %copy-done.2, bf16[128]{0:T(256)(128)(2,1)S(1)} %compare_convert_fusion), kind=kOutput, calls=%fused_computation.24 | convolution fusion | flops 67125248 | bytes 1589504 | tf_op jit(solution)/shard_map/dot_general | solution.py:8
  28.5 0.0 copy-start.5
  28.5 3.8 %fusion.16 = f32[64,64]{1,0:T(8,128)S(1)} fusion(bf16[128,64]{1,0:T(8,128)(2,1)S(1)} %fusion.34, bf16[14336,64]{0,1:T(8,128)(2,1)} %param.38, bf16[1,128,14336]{2,1,0:T(8,128)(2,1)} %param.27), kind=kOutput, calls=%fused_computation.15 | convolution fusion | flops 235937792 | bytes 5537792 | tf_op jit(solution)/shard_map/dot_general | solution.py:12
  32.3 0.1 stack_reshape.27
  32.4 0.8 stack.3
  33.2 0.0 all-gather.6.cloned.1.call-update
  33.3 0.0 copy-done.5
  33.3 47.3 %all-gather.6.cloned.1.call-done = f32[16,7,4096]{2,1,0:T(8,128)} async-done(((f32[1,7,4096]{2,1,0:T(8,128)}), f32[16,7,4096]{2,1,0:T(8,128)}) %all-gather.6.cloned.1.call-update) | async-done | bytes 1835024 | tf_op jit(solution)/shard_map/all_gather | solution.py:19
  80.6 1.7 %reduce.1 = f32[7,4096]{1,0:T(8,128)S(1)} reduce(f32[16,7,4096]{2,1,0:T(8,128)} %all-gather.6.cloned.1.call-done, f32[]{:T(128)} %constant.7.clone.1), dimensions={0}, to_apply=%region_0.0 | reduce | flops 430080 | bytes 1949700 | tf_op jit(solution)/shard_map/reduce_sum | solution.py:19
  82.4 14.5 %all-gather.3 = f32[8,7,256]{2,1,0:T(8,128)S(1)} all-gather(f32[1,7,256]{2,1,0:T(8,128)S(1)} %dynamic-slice_bitcast_fusion), channel_id=3, replica_groups=mesh['dp'=8,'ctx'=16] {'dp'}, dimensions={0}, use_global_device_ids=true | all-gather | bytes 64512 | tf_op jit(solution)/shard_map/all_gather | solution.py:81
  96.9 0.1 multiply_reduce_fusion
  97.0 0.6 broadcast_in_dim.2
  (3 shorter events, 0.0 us)
Async XLA Ops:
  6.5 2.7 %copy-start = (bf16[14336,64]{0,1:T(8,128)(2,1)S(1)}, bf16[14336,64]{0,1:T(8,128)(2,1)}, u32[]{:S(2)}) copy-start(bf16[14336,64]{0,1:T(8,128)(2,1)} %param.44) | copy-start | bytes 5505028
  6.5 74.1 %all-gather.6.cloned.1.call-start = ((), (), s32[]{:S(2)}) async-start(), calls=%async_computation | async-start | bytes 2228224 | tf_op jit(solution)/shard_map/all_gather | solution.py:19
  12.6 4.0 %copy-start.3 = (bf16[4096,64]{0,1:T(8,128)(2,1)S(1)}, bf16[4096,64]{0,1:T(8,128)(2,1)}, u32[]{:S(2)}) copy-start(bf16[4096,64]{0,1:T(8,128)(2,1)} %param.35) | copy-start | bytes 1572868
  16.5 4.9 %copy-start.1 = (bf16[1,128,4096]{2,1,0:T(8,128)(2,1)S(1)}, bf16[1,128,4096]{2,1,0:T(8,128)(2,1)}, u32[]{:S(2)}) copy-start(bf16[1,128,4096]{2,1,0:T(8,128)(2,1)} %param.28) | copy-start | bytes 3145732
  18.4 4.8 %copy-start.4 = (bf16[4096,64]{0,1:T(8,128)(2,1)S(1)}, bf16[4096,64]{0,1:T(8,128)(2,1)}, u32[]{:S(2)}) copy-start(bf16[4096,64]{0,1:T(8,128)(2,1)} %param.36) | copy-start | bytes 1572868
  23.1 3.9 %copy-start.2 = (bf16[1,128,4096]{2,1,0:T(8,128)(2,1)S(1)}, bf16[1,128,4096]{2,1,0:T(8,128)(2,1)}, u32[]{:S(2)}) copy-start(bf16[1,128,4096]{2,1,0:T(8,128)(2,1)} %param.34) | copy-start | bytes 3145732
  28.5 4.8 %copy-start.5 = (s32[8]{0:T(128)S(1)}, s32[8]{0:T(128)}, u32[]{:S(2)}) copy-start(s32[8]{0:T(128)} %param.47) | copy-start | bytes 100
Sparse Core Ops, SparseCore 0:
  33.4 47.1 all-gather.5
